TPU v7x, 32 devices: a whole 2x2x4 slice. The times are simulated.
32 devices in a mesh: groups: 2 (over y), brick: 16 (over z, x, core), frame: 1.
Axes of the slice: x: 2, y: 2, z: 4, core: 2. Of those that a mesh axis runs over, the one named last changes fastest.
Arguments:
- volume: float32 [4, 128, 32, 512], P(('groups', 'frame'), 'brick'), parts along dimension 0, may hold values from -6 to 6
- offsets: int32 [128, 3], P(('groups', 'brick')), parts along dimension 0, may hold values from -8 to 8
Outputs:
- correlation: float32 [128, 32, 32, 32], P(('groups', 'brick', 'frame')), parts along dimension 0
There are 2 independent parts, one for each index of `groups`. A program takes and returns all parts, laid end to end along the dimension named above; each array names one. Nothing has to cross between parts.
All inputs are finite; a program needn't handle non-finite values.
Results may differ from a plain program's by a relative error of at most 0.0003.
Values sent between devices are 32-bit elements; how exact they have to be, the bound alone decides.
A program may use at most 192 MiB of HBM per device.

v0:
```python
import functools

import jax
import jax.numpy as jnp
import ml_dtypes
import numpy as np
from jax import lax
from jax.experimental import pallas as pl
from jax.experimental.pallas import tpu as pltpu
from jax.sharding import PartitionSpec as P

W = 32
H = 8
COLS_DEV = 1
ZB = 4


HIGHEST = lax.Precision.HIGHEST


def from_behind(shard, axis, by):
    count = lax.axis_size(axis)
    pairs = [(i, i + by) for i in range(count) if 0 <= i + by < count]
    return lax.ppermute(shard, axis, pairs)


def taper_table(width):
    position = jnp.arange(width).astype(jnp.float32)
    return 0.5 - 0.5 * jnp.cos(2.0 * jnp.pi * (position + 0.5) / width)


def fourier_tables(width):
    index = jnp.arange(width)
    product = index[:, None] * index[None, :] % width
    angle = 2.0 * jnp.pi * product.astype(jnp.float32) / width
    return (jnp.cos(angle), jnp.sin(angle))


def plane_tables(width):
    index = jnp.arange(width * width)
    upper = index // width
    lower = index % width
    product = (upper[:, None] * upper[None, :] + lower[:, None] * lower[None, :]) % width
    angle = 2.0 * jnp.pi * product.astype(jnp.float32) / width
    return (jnp.cos(angle), jnp.sin(angle))


def depth_apply(table, values):
    return jnp.einsum("kz,nzm->nkm", table, values, precision=HIGHEST)


def plane_apply(values, table):
    count, depth, plane = values.shape
    flat = values.reshape(count * depth, plane)
    result = jnp.dot(flat, table, precision=HIGHEST, preferred_element_type=jnp.float32)
    return result.reshape(count, depth, plane)


def forward(field, tables):
    cosine, sine, plane_cos, plane_sin = tables
    count, width = (field.shape[0], field.shape[1])
    values = field.reshape(count, width, width * width)
    real_part = plane_apply(values, plane_cos)
    imag_part = -plane_apply(values, plane_sin)
    return (
        depth_apply(cosine, real_part) + depth_apply(sine, imag_part),
        depth_apply(cosine, imag_part) - depth_apply(sine, real_part),
    )


def inverse_real(real_part, imag_part, tables):
    cosine, sine, plane_cos, plane_sin = tables
    first_re = depth_apply(cosine, real_part) - depth_apply(sine, imag_part)
    first_im = depth_apply(cosine, imag_part) + depth_apply(sine, real_part)
    result = plane_apply(first_re, plane_cos) - plane_apply(first_im, plane_sin)
    width = result.shape[1]
    return result.reshape(result.shape[0], width, width, width)


def column_pieces(slabs):
    count, planes, rows, cols = slabs.shape
    span = COLS_DEV * W
    tiles = slabs.reshape(count, planes, rows // W, W, cols // span, span)
    tiles = jnp.pad(tiles, ((0, 0), (0, 0), (1, 1), (0, 0), (1, 1), (0, 0)))
    tall = jnp.concatenate([tiles[:, :, :-2, W - H :], tiles[:, :, 1:-1], tiles[:, :, 2:, :H]], 3)
    wide = jnp.concatenate(
        [tall[:, :, :, :, :-2, span - H :], tall[:, :, :, :, 1:-1], tall[:, :, :, :, 2:, :H]], 5
    )
    wide = jnp.transpose(wide, (0, 1, 2, 4, 3, 5))
    owners = rows // W * (cols // span)
    return wide.reshape(count, planes, owners, (W + 2 * H) * (span + 2 * H))


def merge_depth(received):
    count = received.shape[0]
    depth_total = received.shape[1] * received.shape[2]
    merged = received.reshape(count, depth_total, W + 2 * H, COLS_DEV * W + 2 * H)
    return jnp.pad(merged, ((0, 0), (H, H), (0, 0), (0, 0)))


def cross_sum(first, paired):
    first_re, first_im = first
    paired_re, paired_im = paired
    spectrum_re = jnp.sum(first_re * paired_re + first_im * paired_im, axis=0)
    spectrum_im = jnp.sum(first_re * paired_im - first_im * paired_re, axis=0)
    return (spectrum_re, spectrum_im)


def shards(volume, offsets):
    frames_here = volume.shape[0]
    taper = taper_table(W)
    weight3 = taper[:, None, None] * taper[None, :, None] * taper[None, None, :]
    cosine, sine = fourier_tables(W)
    plane_cos, plane_sin = plane_tables(W)
    tables = (cosine, sine, plane_cos, plane_sin)
    factor = 4.0 / W**1.5 / W**3

    def transformed(fields, moves, depth_rel, col_rel):

        def windows(frame_field):

            def one_window(depth, column, move):
                return lax.dynamic_slice(
                    frame_field,
                    (H + depth * W + move[0], H + move[1], H + column * W + move[2]),
                    (W, W, W),
                )

            return jax.vmap(one_window)(depth_rel, col_rel, moves) * weight3

        cut = jax.vmap(windows)(fields)
        frame_total, count = (cut.shape[0], cut.shape[1])
        real_part, imag_part = forward(cut.reshape(frame_total * count, W, W, W), tables)
        return (
            real_part.reshape(frame_total, count, W, W * W),
            imag_part.reshape(frame_total, count, W, W * W),
        )

    columns = lax.all_to_all(
        column_pieces(volume), "brick", split_axis=2, concat_axis=1, tiled=True
    )
    following = from_behind(columns, "frame", -1)
    stacked = jnp.concatenate([columns, following], 0)
    stacked = merge_depth(stacked)
    local_count = offsets.shape[0]
    local_index = jnp.arange(local_count)
    depth_index = local_index % ZB
    column_local = local_index // ZB
    first = transformed(stacked[:frames_here], jnp.zeros_like(offsets), depth_index, column_local)
    second_re, second_im = transformed(stacked[1:], offsets, depth_index, column_local)
    paired_re = second_re[:-1] + second_re[1:]
    paired_im = second_im[:-1] + second_im[1:]
    spectrum_re, spectrum_im = cross_sum(first, (paired_re, paired_im))
    share_re, share_im = (
        lax.psum_scatter(spectrum_re, "frame", scatter_dimension=0, tiled=True),
        lax.psum_scatter(spectrum_im, "frame", scatter_dimension=0, tiled=True),
    )
    return inverse_real(share_re, share_im, tables) * factor


KB = 3
T = 8


def halves(table):
    table = np.asarray(table, np.float32)
    high = table.astype(ml_dtypes.bfloat16)
    low = (table - high.astype(np.float32)).astype(ml_dtypes.bfloat16)
    return np.stack([high, low])


def fixed_tables():
    index = np.arange(W)
    angle = 2.0 * np.pi * (index[:, None] * index[None, :] % W) / W
    cosine, sine = np.cos(angle), np.sin(angle)
    unit = np.eye(T)
    kept = np.zeros((KB * T, W))
    kept[: W // 2 + 1, : W // 2 + 1] = np.eye(W // 2 + 1)
    parts = np.stack([kept @ cosine, -(kept @ sine)]).reshape(2, KB, T, W)
    along_y = np.einsum("rbky,zs->rbzksy", parts, unit).reshape(2 * KB * T * T, T * W)
    weight = np.where((index == 0) | (index == W // 2), 1.0, 2.0)[:, None]
    factor = 4.0 / W**1.5 / W**3
    parts = factor * np.stack([kept @ (weight * cosine), -(kept @ (weight * sine))]).reshape(2, KB, T, W)
    back_y = np.einsum("rbky,zs->zyrbsk", parts, unit).reshape(T * W, 2 * KB * T * T)
    along_z = np.kron(np.block([[cosine, sine], [-sine, cosine]]), unit)
    four = np.eye(ZB)
    along_x = np.block([[np.kron(four, cosine), -np.kron(four, sine)], [np.kron(four, sine), np.kron(four, cosine)]])
    taper = 0.5 - 0.5 * np.cos(2.0 * np.pi * (index + 0.5) / W)
    lanes = np.tile(taper, ZB)
    weight3 = (taper[:, None, None] * taper[None, :, None] * lanes[None, None, :]).astype(np.float32)
    lane = np.arange(128)
    brick = np.arange(ZB)[:, None]
    main = (brick * 4 + lane // W) * 64 + lane % W + H
    edge = lane % 16
    halo = (brick * 4 + lane % 64 // 16) * 64 + np.where(edge < H, edge, edge + W)
    row_key = np.concatenate([main.reshape(-1), halo.reshape(-1)]).astype(np.int32)[:, None]
    return (
        halves(along_y), halves(along_z), halves(along_x),
        halves(along_x.T), halves(along_z.T), halves(back_y),
        weight3, row_key,
    )


def split(values):
    high = values.astype(jnp.bfloat16)
    return high, (values - high.astype(jnp.float32)).astype(jnp.bfloat16)


def mul(left, right):
    return jnp.dot(left, right, preferred_element_type=jnp.float32)


def from_left(table, values):
    high, low = split(values)
    return mul(table[0], high) + mul(table[0], low) + mul(table[1], high)


def from_right(values, table):
    high, low = split(values)
    return mul(high, table[0]) + mul(low, table[0]) + mul(high, table[1])


def pack(volume, send):
    columns = send.shape[0]
    for c in range(columns):
        at = c * W
        for f in range(2):
            parts = [volume[f, :, T * j : T * j + T, at : at + W] for j in range(4)]
            send[c, T * f : T * f + T] = jnp.concatenate(parts, -1)
        parts = []
        for zh in range(2):
            for j in range(4):
                for start in (at - H, at + W):
                    if 0 <= start < columns * W:
                        parts.append(volume[1, 4 * zh : 4 * zh + 4, T * j : T * j + T, start : start + H])
                    else:
                        parts.append(jnp.zeros((4, T, H), jnp.float32))
        send[c, 2 * T :] = jnp.concatenate(parts, -1)


def first_windows(held, row_key, field):
    lane = lax.broadcasted_iota(jnp.int32, (1, 4 * 128), 1)
    col_key = (lane // W % 4 * 4 + lane // 128) * 64 + lane % W + H
    chosen = (row_key[0:512] == col_key).astype(jnp.float32).astype(jnp.bfloat16)
    rows = jnp.concatenate([held[4 * q : 4 * q + 4, 0:T].reshape(W * T, 128) for q in range(ZB)], -1)
    high, low = split(rows)
    moved = mul(high, chosen) + mul(low, chosen)
    for j in range(4):
        field[:, T * j : T * j + T, 0:128] = moved[:, 128 * j : 128 * j + 128].reshape(W, T, 128)


def second_windows(held, offsets, row_key, main, halo, spread, field):
    lane = lax.broadcasted_iota(jnp.int32, (1, 4 * 128), 1)
    brick = lane // W % 4
    shift = jnp.zeros((1, 4 * 128), jnp.int32)
    for q in range(ZB):
        shift = jnp.where(brick == q, offsets[q, 2], shift)
    col_key = (brick * 4 + lane // 128) * 64 + lane % W + H + shift
    chosen = (row_key[...] == col_key).astype(jnp.float32).astype(jnp.bfloat16)
    depth = main.shape[0] - 2 * H
    for ref in (main, halo):
        ref[0:H] = jnp.zeros((H, T, 128), jnp.float32)
        ref[H + depth :] = jnp.zeros((H, T, 128), jnp.float32)
    upper = lax.broadcasted_iota(jnp.int32, (1, 1, 1, 128), 3) >= 64
    slabs = held.shape[0]
    main[H : H + depth] = held[:, T : 2 * T].reshape(depth, T, 128)
    edges = held[:, 2 * T :]
    both = jnp.concatenate([jnp.where(upper, 0.0, edges), jnp.where(upper, edges, 0.0)], 1)
    halo[H : H + depth] = both.reshape(depth, T, 128)
    span = W + 2 * H
    rows = [ref[W * q : W * q + span].reshape(span * T, 128) for ref in (main, halo) for q in range(ZB)]
    high, low = split(jnp.concatenate(rows, -1))
    moved = mul(high, chosen) + mul(low, chosen)
    spread[:, 0:H] = jnp.zeros((span, H, 128), jnp.float32)
    spread[:, H + W :] = jnp.zeros((span, H, 128), jnp.float32)
    for j in range(4):
        spread[:, H + T * j : H + T * j + T] = moved[:, 128 * j : 128 * j + 128].reshape(span, T, 128)
    own = lax.broadcasted_iota(jnp.int32, (1, 1, 128), 2) // W
    cut = jnp.zeros((W, W, 128), jnp.float32)
    for q in range(ZB):
        window = spread[pl.ds(H + offsets[q, 0], W), pl.ds(H + offsets[q, 1], W), :]
        cut = jnp.where(own == q, window, cut)
    field[:, :, 128:256] = cut


def correlate(field, weight3, tables, mid, back, out):
    along_y, along_z, along_x, back_x, back_z, back_y = tables
    block = T * T
    for zb in range(4):
        weight = weight3[T * zb : T * zb + T]
        tapered = field[T * zb : T * zb + T] * jnp.concatenate([weight, weight], -1)
        part = from_left(along_y, tapered.reshape(T * W, 256))
        for r in range(2):
            for b in range(KB):
                at = (r * KB + b) * block
                mid[b, (r * 4 + zb) * block : (r * 4 + zb + 1) * block] = part[at : at + block]
    half = W * T
    for b in range(KB):
        spec = from_left(along_z, mid[b])
        first, second = (
            from_right(jnp.concatenate([spec[:half, s], spec[half:, s]], -1), along_x)
            for s in (slice(0, 128), slice(128, 256))
        )
        first_re, first_im = first[:, :128], first[:, 128:]
        second_re, second_im = second[:, :128], second[:, 128:]
        real_part = first_re * second_re + first_im * second_im
        imag_part = first_re * second_im - first_im * second_re
        lines = from_right(jnp.concatenate([real_part, imag_part], -1), back_x)
        part = from_left(back_z, jnp.concatenate([lines[:, :128], lines[:, 128:]], 0))
        for r in range(2):
            for zb in range(4):
                at = (r * 4 + zb) * block
                back[zb, (r * KB + b) * block : (r * KB + b + 1) * block] = part[at : at + block]
    for zb in range(4):
        result = from_left(back_y, back[zb]).reshape(T, W, 128)
        for q in range(ZB):
            out[q, T * zb : T * zb + T] = result[:, :, W * q : W * q + W]


def bricks(offsets, held, along_y, along_z, along_x, back_x, back_z, back_y, weight3, row_key, out,
           main, halo, spread, field, mid, back):
    first_windows(held, row_key, field)
    second_windows(held, offsets, row_key, main, halo, spread, field)
    correlate(field, weight3, (along_y, along_z, along_x, back_x, back_z, back_y), mid, back, out)


def two_frames(volume, offsets):
    slabs = lax.axis_size("brick")
    planes = volume.shape[1]
    depth = slabs * planes
    rows = 2 * planes + planes // 2
    vmem = pl.BlockSpec(memory_space=pltpu.VMEM)
    send = pl.pallas_call(
        pack,
        out_shape=jax.ShapeDtypeStruct((slabs, rows, T, 128), jnp.float32),
        in_specs=[vmem],
        out_specs=vmem,
        compiler_params=pltpu.CompilerParams(vmem_limit_bytes=32 << 20),
    )(volume)
    held = lax.all_to_all(send, "brick", split_axis=0, concat_axis=0, tiled=True)
    tables = fixed_tables()
    return pl.pallas_call(
        bricks,
        out_shape=jax.ShapeDtypeStruct((ZB, W, W, W), jnp.float32),
        in_specs=[pl.BlockSpec(memory_space=pltpu.SMEM)] + [vmem] * (1 + len(tables)),
        out_specs=vmem,
        scratch_shapes=[
            pltpu.VMEM((depth + 2 * H, T, 128), jnp.float32),
            pltpu.VMEM((depth + 2 * H, T, 128), jnp.float32),
            pltpu.VMEM((W + 2 * H, W + 2 * H, 128), jnp.float32),
            pltpu.VMEM((W, W, 256), jnp.float32),
            pltpu.VMEM((KB, 2 * W * T, 256), jnp.float32),
            pltpu.VMEM((4, 2 * KB * T * T, 128), jnp.float32),
        ],
        compiler_params=pltpu.CompilerParams(vmem_limit_bytes=48 << 20),
    )(offsets, held, *[jnp.asarray(t) for t in tables])


def per_device(volume, offsets):
    slabs = lax.axis_size("brick")
    frames, planes, rows, cols = volume.shape
    short = lax.axis_size("frame") == 1 and frames == 2 and planes == T and rows == W
    if short and cols == slabs * W and slabs * planes == ZB * W and offsets.shape[0] == ZB:
        return two_frames(volume, offsets)
    return shards(volume, offsets)


def solution(mesh):
    return jax.shard_map(
        per_device,
        mesh=mesh,
        in_specs=(P(("groups", "frame"), "brick", None, None), P(("groups", "brick"), None)),
        out_specs=P(("groups", "brick", "frame"), None, None, None),
        check_vma=False,
    )
```

profile of v0, /device:TPU:0, one launch (start us, length us, event | category | flops | bytes accessed | tf_op | source)
XLA Modules:
  0.0 52.7 jit_solution(6782114524981749503)
XLA Ops:
  0.0 0.0 copy-start.2
  0.0 1.2 %copy-done.2 = f32[2,8,32,512]{3,2,1,0:T(8,128)S(1)} copy-done((f32[2,8,32,512]{3,2,1,0:T(8,128)S(1)}, f32[2,8,32,512]{3,2,1,0:T(8,128)}, u32[]{:S(2)}) %copy-start.2) | copy-done | bytes 1048600
  1.2 0.0 copy-start.4
  1.2 0.0 copy-start.5
  1.2 0.0 copy-start.6
  1.2 0.0 copy-start.7
  1.2 0.0 copy-start.8
  1.2 0.0 copy-start.9
  1.3 1.9 %shard_map.100 = f32[16,20,8,128]{3,2,1,0:T(8,128)S(1)} custom-call(f32[2,8,32,512]{3,2,1,0:T(8,128)S(1)} %copy-done.2), custom_call_target="tpu_custom_call" | custom-call | tf_op jit(solution)/shard_map/pallas_call | solution.py:333
  3.2 0.0 copy-start
  3.2 0.0 copy-start.1
  3.2 0.0 copy-start.3
  3.2 38.8 %all_to_all.5.held = f32[16,20,8,128]{3,2,1,0:T(8,128)S(1)} all-to-all(f32[16,20,8,128]{3,2,1,0:T(8,128)S(1)} %shard_map.100), channel_id=1, replica_groups=mesh['groups'=2,'brick'=16,'frame'=1] {'brick'}, dimensions={0} | all-to-all | bytes 2621440 | tf_op jit(solution)/shard_map/all_to_all | solution.py:340
  42.0 0.0 copy-done.4
  42.0 0.0 copy-done.5
  42.0 0.0 copy-done.6
  42.0 0.0 copy-done.7
  42.0 0.0 copy-done.8
  42.0 0.0 copy-done.9
  42.0 0.0 copy-done
  42.0 0.0 copy-done.1
  42.1 0.0 copy-done.3
  42.1 10.7 %shard_map.101 = f32[4,32,32,32]{3,2,1,0:T(8,128)} custom-call(s32[4,3]{1,0:T(4,128)S(1)} %copy-done.9, f32[16,20,8,128]{3,2,1,0:T(8,128)S(1)} %all_to_all.5.held, bf16[2,384,256]{2,1,0:T(8,128)(2,1)S(1)} %copy-done.6, bf16[2,512,512]{2,1,0:T(8,128)(2,1)S(1)} %copy-done.1, bf16[2,256,256]{2,1,0:T(8,128)(2,1)S(1)} %copy-done.8, ...), custom_call_target="tpu_custom_call" | custom-call | tf_op jit(solution)/shard_map/pallas_call | solution.py:342
Async XLA Ops:
  0.0 1.2 %copy-start.2 = (f32[2,8,32,512]{3,2,1,0:T(8,128)S(1)}, f32[2,8,32,512]{3,2,1,0:T(8,128)}, u32[]{:S(2)}) copy-start(f32[2,8,32,512]{3,2,1,0:T(8,128)} %volume.1) | copy-start | bytes 3145732
  1.2 40.8 %copy-start.4 = (f32[32,32,128]{2,1,0:T(8,128)S(1)}, f32[32,32,128]{2,1,0:T(8,128)}, u32[]{:S(2)}) copy-start(f32[32,32,128]{2,1,0:T(8,128)} %constant.22.clone.weight3) | copy-start | bytes 1572868
  1.2 40.8 %copy-start.5 = (bf16[2,256,384]{2,1,0:T(8,128)(2,1)S(1)}, bf16[2,256,384]{2,1,0:T(8,128)(2,1)}, u32[]{:S(2)}) copy-start(bf16[2,256,384]{2,1,0:T(8,128)(2,1)} %constant.21.clone.back_y) | copy-start | bytes 1179652
  1.2 40.8 %copy-start.6 = (bf16[2,384,256]{2,1,0:T(8,128)(2,1)S(1)}, bf16[2,384,256]{2,1,0:T(8,128)(2,1)}, u32[]{:S(2)}) copy-start(bf16[2,384,256]{2,1,0:T(8,128)(2,1)} %constant.16.clone.along_y) | copy-start | bytes 1179652
  1.2 40.8 %copy-start.7 = (bf16[2,256,256]{2,1,0:T(8,128)(2,1)S(1)}, bf16[2,256,256]{2,1,0:T(8,128)(2,1)}, u32[]{:S(2)}) copy-start(bf16[2,256,256]{2,1,0:T(8,128)(2,1)} %constant.19.clone.back_x) | copy-start | bytes 786436
  1.2 40.8 %copy-start.8 = (bf16[2,256,256]{2,1,0:T(8,128)(2,1)S(1)}, bf16[2,256,256]{2,1,0:T(8,128)(2,1)}, u32[]{:S(2)}) copy-start(bf16[2,256,256]{2,1,0:T(8,128)(2,1)} %constant.18.clone.along_x) | copy-start | bytes 786436
  1.2 40.8 %copy-start.9 = (s32[4,3]{1,0:T(4,128)S(1)}, s32[4,3]{1,0:T(4,128)}, u32[]{:S(2)}) copy-start(s32[4,3]{1,0:T(4,128)} %offsets.1) | copy-start | bytes 148
  3.2 38.9 %copy-start = (bf16[2,512,512]{2,1,0:T(8,128)(2,1)S(1)}, bf16[2,512,512]{2,1,0:T(8,128)(2,1)}, u32[]{:S(2)}) copy-start(bf16[2,512,512]{2,1,0:T(8,128)(2,1)} %constant.20.clone.back_z) | copy-start | bytes 3145732
  3.2 38.9 %copy-start.1 = (bf16[2,512,512]{2,1,0:T(8,128)(2,1)S(1)}, bf16[2,512,512]{2,1,0:T(8,128)(2,1)}, u32[]{:S(2)}) copy-start(bf16[2,512,512]{2,1,0:T(8,128)(2,1)} %constant.17.clone.along_z) | copy-start | bytes 3145732
  3.2 38.9 %copy-start.3 = (s32[1024,1]{1,0:T(8,128)S(1)}, s32[1024,1]{1,0:T(8,128)}, u32[]{:S(2)}) copy-start(s32[1024,1]{1,0:T(8,128)} %constant.23.clone.row_key) | copy-start | bytes 12292
where the time goes:
time: 53.2 us; the launch traced here: 52.7 us
  blocking collectives  38.8 us (73%)
  Pallas kernels  12.5 us (23%)
  local copies, waits for them, and re-layouts  1.27 us (2%)
    all_to_all x1, blocking collectives, two_frames(): lax.all_to_all(send, 'brick', split_axis=0, concat_axis=0, tiled=True)  38.8 us
    pallas_call x1, Pallas kernels, two_frames(): pl.pallas_call(bricks, out_shape=jax.ShapeDtypeStruct((ZB, W, W, W), jnp....  10.7 us
    pallas_call x1, Pallas kernels, two_frames(): pl.pallas_call(pack, out_shape=jax.ShapeDtypeStruct((slabs, rows, T, 128)...  1.88 us
    unnamed x20, local copies, waits for them, and re-layouts  1.27 us

commit v1 on v0

--- a/solution.py
+++ b/solution.py
@@ -220,13 +220,19 @@
     return mul(high, table[0]) + mul(low, table[0]) + mul(high, table[1])
 
 
-def pack(volume, send):
+def pack_first(volume, send):
+    for c in range(send.shape[0]):
+        at = c * W
+        parts = [volume[0, :, T * j : T * j + T, at : at + W] for j in range(4)]
+        send[c] = jnp.concatenate(parts, -1)
+
+
+def pack_second(volume, send):
     columns = send.shape[0]
     for c in range(columns):
         at = c * W
-        for f in range(2):
-            parts = [volume[f, :, T * j : T * j + T, at : at + W] for j in range(4)]
-            send[c, T * f : T * f + T] = jnp.concatenate(parts, -1)
+        parts = [volume[1, :, T * j : T * j + T, at : at + W] for j in range(4)]
+        send[c, 0:T] = jnp.concatenate(parts, -1)
         parts = []
         for zh in range(2):
             for j in range(4):
@@ -235,18 +241,18 @@
                         parts.append(volume[1, 4 * zh : 4 * zh + 4, T * j : T * j + T, start : start + H])
                     else:
                         parts.append(jnp.zeros((4, T, H), jnp.float32))
-        send[c, 2 * T :] = jnp.concatenate(parts, -1)
+        send[c, T:] = jnp.concatenate(parts, -1)
 
 
 def first_windows(held, row_key, field):
     lane = lax.broadcasted_iota(jnp.int32, (1, 4 * 128), 1)
     col_key = (lane // W % 4 * 4 + lane // 128) * 64 + lane % W + H
     chosen = (row_key[0:512] == col_key).astype(jnp.float32).astype(jnp.bfloat16)
-    rows = jnp.concatenate([held[4 * q : 4 * q + 4, 0:T].reshape(W * T, 128) for q in range(ZB)], -1)
+    rows = jnp.concatenate([held[4 * q : 4 * q + 4].reshape(W * T, 128) for q in range(ZB)], -1)
     high, low = split(rows)
     moved = mul(high, chosen) + mul(low, chosen)
     for j in range(4):
-        field[:, T * j : T * j + T, 0:128] = moved[:, 128 * j : 128 * j + 128].reshape(W, T, 128)
+        field[:, T * j : T * j + T, :] = moved[:, 128 * j : 128 * j + 128].reshape(W, T, 128)
 
 
 def second_windows(held, offsets, row_key, main, halo, spread, field):
@@ -262,9 +268,8 @@
         ref[0:H] = jnp.zeros((H, T, 128), jnp.float32)
         ref[H + depth :] = jnp.zeros((H, T, 128), jnp.float32)
     upper = lax.broadcasted_iota(jnp.int32, (1, 1, 1, 128), 3) >= 64
-    slabs = held.shape[0]
-    main[H : H + depth] = held[:, T : 2 * T].reshape(depth, T, 128)
-    edges = held[:, 2 * T :]
+    main[H : H + depth] = held[:, 0:T].reshape(depth, T, 128)
+    edges = held[:, T:]
     both = jnp.concatenate([jnp.where(upper, 0.0, edges), jnp.where(upper, edges, 0.0)], 1)
     halo[H : H + depth] = both.reshape(depth, T, 128)
     span = W + 2 * H
@@ -280,28 +285,77 @@
     for q in range(ZB):
         window = spread[pl.ds(H + offsets[q, 0], W), pl.ds(H + offsets[q, 1], W), :]
         cut = jnp.where(own == q, window, cut)
-    field[:, :, 128:256] = cut
-
-
-def correlate(field, weight3, tables, mid, back, out):
-    along_y, along_z, along_x, back_x, back_z, back_y = tables
+    field[...] = cut
+
+
+def to_depth(field, weight3, along_y, mid):
     block = T * T
     for zb in range(4):
-        weight = weight3[T * zb : T * zb + T]
-        tapered = field[T * zb : T * zb + T] * jnp.concatenate([weight, weight], -1)
-        part = from_left(along_y, tapered.reshape(T * W, 256))
+        tapered = field[T * zb : T * zb + T] * weight3[T * zb : T * zb + T]
+        part = from_left(along_y, tapered.reshape(T * W, 128))
         for r in range(2):
             for b in range(KB):
                 at = (r * KB + b) * block
                 mid[b, (r * 4 + zb) * block : (r * 4 + zb + 1) * block] = part[at : at + block]
+
+
+def to_spectrum(lines, along_z, along_x):
     half = W * T
+    spec = from_left(along_z, lines)
+    return from_right(jnp.concatenate([spec[:half], spec[half:]], -1), along_x)
+
+
+def exchange(volume, along_y, along_z, along_x, weight3, row_key, spectrum, held_second,
+             send_first, send_second, held_first, field, mid, send_sem, recv_sem):
+    count = send_first.shape[0]
+    me = lax.axis_index("brick")
+    steps = sorted(range(1, count), key=lambda k: (abs(k - count // 2), k))
+    barrier = pltpu.get_barrier_semaphore()
+    for k in steps:
+        pl.semaphore_signal(
+            barrier, inc=1, device_id={"brick": lax.rem(me + k, count)}, device_id_type=pl.DeviceIdType.MESH
+        )
+    pack_first(volume, send_first)
+    pl.semaphore_wait(barrier, count - 1)
+
+    def start(f, send, held):
+        copies = []
+        for k in steps:
+            to = lax.rem(me + k, count)
+            copy = pltpu.make_async_remote_copy(
+                src_ref=send.at[to],
+                dst_ref=held.at[me],
+                send_sem=send_sem.at[f, k],
+                recv_sem=recv_sem.at[f, k],
+                device_id={"brick": to},
+                device_id_type=pl.DeviceIdType.MESH,
+            )
+            copy.start()
+            copies.append(copy)
+        held[pl.ds(me, 1)] = send[pl.ds(me, 1)]
+        return copies
+
+    early = start(0, send_first, held_first)
+    pack_second(volume, send_second)
+    late = start(1, send_second, held_second)
+    for copy in early:
+        copy.wait()
+    first_windows(held_first, row_key, field)
+    to_depth(field, weight3, along_y, mid)
     for b in range(KB):
-        spec = from_left(along_z, mid[b])
-        first, second = (
-            from_right(jnp.concatenate([spec[:half, s], spec[half:, s]], -1), along_x)
-            for s in (slice(0, 128), slice(128, 256))
-        )
-        first_re, first_im = first[:, :128], first[:, 128:]
+        spectrum[b] = to_spectrum(mid[b], along_z, along_x)
+    for copy in late:
+        copy.wait()
+
+
+def correlate(offsets, first, held, along_y, along_z, along_x, back_x, back_z, back_y, weight3, row_key, out,
+              main, halo, spread, field, mid, back):
+    second_windows(held, offsets, row_key, main, halo, spread, field)
+    to_depth(field, weight3, along_y, mid)
+    block = T * T
+    for b in range(KB):
+        second = to_spectrum(mid[b], along_z, along_x)
+        first_re, first_im = first[b, :, :128], first[b, :, 128:]
         second_re, second_im = second[:, :128], second[:, 128:]
         real_part = first_re * second_re + first_im * second_im
         imag_part = first_re * second_im - first_im * second_re
@@ -317,43 +371,51 @@
             out[q, T * zb : T * zb + T] = result[:, :, W * q : W * q + W]
 
 
-def bricks(offsets, held, along_y, along_z, along_x, back_x, back_z, back_y, weight3, row_key, out,
-           main, halo, spread, field, mid, back):
-    first_windows(held, row_key, field)
-    second_windows(held, offsets, row_key, main, halo, spread, field)
-    correlate(field, weight3, (along_y, along_z, along_x, back_x, back_z, back_y), mid, back, out)
-
-
 def two_frames(volume, offsets):
     slabs = lax.axis_size("brick")
     planes = volume.shape[1]
     depth = slabs * planes
-    rows = 2 * planes + planes // 2
+    rows = planes + planes // 2
     vmem = pl.BlockSpec(memory_space=pltpu.VMEM)
-    send = pl.pallas_call(
-        pack,
-        out_shape=jax.ShapeDtypeStruct((slabs, rows, T, 128), jnp.float32),
-        in_specs=[vmem],
-        out_specs=vmem,
-        compiler_params=pltpu.CompilerParams(vmem_limit_bytes=32 << 20),
-    )(volume)
-    held = lax.all_to_all(send, "brick", split_axis=0, concat_axis=0, tiled=True)
-    tables = fixed_tables()
+    along_y, along_z, along_x, back_x, back_z, back_y, weight3, row_key = map(jnp.asarray, fixed_tables())
+    field = pltpu.VMEM((W, W, 128), jnp.float32)
+    mid = pltpu.VMEM((KB, 2 * W * T, 128), jnp.float32)
+    first, held = pl.pallas_call(
+        exchange,
+        out_shape=[
+            jax.ShapeDtypeStruct((KB, W * T, 256), jnp.float32),
+            jax.ShapeDtypeStruct((slabs, rows, T, 128), jnp.float32),
+        ],
+        in_specs=[vmem] * 6,
+        out_specs=[vmem] * 2,
+        scratch_shapes=[
+            pltpu.VMEM((slabs, planes, T, 128), jnp.float32),
+            pltpu.VMEM((slabs, rows, T, 128), jnp.float32),
+            pltpu.VMEM((slabs, planes, T, 128), jnp.float32),
+            field,
+            mid,
+            pltpu.SemaphoreType.DMA((2, slabs)),
+            pltpu.SemaphoreType.DMA((2, slabs)),
+        ],
+        compiler_params=pltpu.CompilerParams(
+            collective_id=0, has_side_effects=True, vmem_limit_bytes=32 << 20
+        ),
+    )(volume, along_y, along_z, along_x, weight3, row_key[:512])
     return pl.pallas_call(
-        bricks,
+        correlate,
         out_shape=jax.ShapeDtypeStruct((ZB, W, W, W), jnp.float32),
-        in_specs=[pl.BlockSpec(memory_space=pltpu.SMEM)] + [vmem] * (1 + len(tables)),
+        in_specs=[pl.BlockSpec(memory_space=pltpu.SMEM)] + [vmem] * 10,
         out_specs=vmem,
         scratch_shapes=[
             pltpu.VMEM((depth + 2 * H, T, 128), jnp.float32),
             pltpu.VMEM((depth + 2 * H, T, 128), jnp.float32),
             pltpu.VMEM((W + 2 * H, W + 2 * H, 128), jnp.float32),
-            pltpu.VMEM((W, W, 256), jnp.float32),
-            pltpu.VMEM((KB, 2 * W * T, 256), jnp.float32),
+            field,
+            mid,
             pltpu.VMEM((4, 2 * KB * T * T, 128), jnp.float32),
         ],
-        compiler_params=pltpu.CompilerParams(vmem_limit_bytes=48 << 20),
-    )(offsets, held, *[jnp.asarray(t) for t in tables])
+        compiler_params=pltpu.CompilerParams(vmem_limit_bytes=32 << 20),
+    )(offsets, first, held, along_y, along_z, along_x, back_x, back_z, back_y, weight3, row_key)
 
 
 def per_device(volume, offsets):

time: 53.2 us -> 53.1 us (level)
  blocking collectives: 38.8 us -> 0 us
  Pallas kernels: 12.5 us -> 44.3 us
  local copies, waits for them, and re-layouts: 1.27 us -> 8.35 us
    all_to_all x1 -> x0, blocking collectives: 38.8 us -> none  [two_frames(): lax.all_to_all(send, 'brick', split_axis=0, concat_axis=0, tiled=True)]
    pallas_call x2, Pallas kernels: 12.5 us -> 44.3 us  [the longest x1 34.2 us: two_frames(): pl.pallas_call(exchange, out_shape=[jax.ShapeDtypeStruct((KB, W * T, 256)...]
    unnamed x20 -> x28, local copies, waits for them, and re-layouts: 1.27 us -> 8.35 us
where the time goes in v1:
time: 53.1 us; the launch traced here: 52.7 us
  Pallas kernels  44.3 us (83%)
  local copies, waits for them, and re-layouts  8.35 us (16%)
    pallas_call x1, Pallas kernels, two_frames(): pl.pallas_call(exchange, out_shape=[jax.ShapeDtypeStruct((KB, W * T, 256)...  34.2 us
    pallas_call x1, Pallas kernels, two_frames(): pl.pallas_call(correlate, out_shape=jax.ShapeDtypeStruct((ZB, W, W, W), j...  10.1 us
    unnamed x28, local copies, waits for them, and re-layouts  8.35 us

profile of v1, /device:TPU:0, one launch (start us, length us, event | category | flops | bytes accessed | tf_op | source)
XLA Modules:
  0.0 52.7 jit_solution(552628105715575468)
XLA Ops:
  0.0 0.0 copy-start
  0.0 1.2 %copy-done = bf16[2,512,512]{2,1,0:T(8,128)(2,1)S(1)} copy-done((bf16[2,512,512]{2,1,0:T(8,128)(2,1)S(1)}, bf16[2,512,512]{2,1,0:T(8,128)(2,1)}, u32[]{:S(2)}) %copy-start) | copy-done | bytes 1048600
  1.2 0.0 copy-start.2
  1.2 1.0 %copy-done.2 = f32[32,32,128]{2,1,0:T(8,128)S(1)} copy-done((f32[32,32,128]{2,1,0:T(8,128)S(1)}, f32[32,32,128]{2,1,0:T(8,128)}, u32[]{:S(2)}) %copy-start.2) | copy-done | bytes 524312
  2.3 0.0 copy-start.4
  2.3 1.0 %copy-done.4 = bf16[2,384,256]{2,1,0:T(8,128)(2,1)S(1)} copy-done((bf16[2,384,256]{2,1,0:T(8,128)(2,1)S(1)}, bf16[2,384,256]{2,1,0:T(8,128)(2,1)}, u32[]{:S(2)}) %copy-start.4) | copy-done | bytes 393240
  3.3 0.0 copy-start.5
  3.3 1.2 %copy-done.5 = f32[2,8,32,512]{3,2,1,0:T(8,128)S(1)} copy-done((f32[2,8,32,512]{3,2,1,0:T(8,128)S(1)}, f32[2,8,32,512]{3,2,1,0:T(8,128)}, u32[]{:S(2)}) %copy-start.5) | copy-done | bytes 1048600
  4.5 0.0 copy-start.7
  4.5 0.9 %copy-done.7 = bf16[2,256,256]{2,1,0:T(8,128)(2,1)S(1)} copy-done((bf16[2,256,256]{2,1,0:T(8,128)(2,1)S(1)}, bf16[2,256,256]{2,1,0:T(8,128)(2,1)}, u32[]{:S(2)}) %copy-start.7) | copy-done | bytes 262168
  5.4 0.9 %copy-done.12 = s32[512,1]{1,0:T(8,128)S(1)} copy-done((s32[512,1]{1,0:T(8,128)S(1)}, s32[512,1]{1,0:T(8,128)}, u32[]{:S(2)}) %copy-start.12) | copy-done | bytes 2072
  6.4 0.0 copy-start.9
  6.4 0.0 copy-start.13
  6.4 34.2 %shard_map.100 = (f32[3,256,256]{2,1,0:T(8,128)S(1)}, f32[16,12,8,128]{3,2,1,0:T(8,128)S(1)}) custom-call(f32[2,8,32,512]{3,2,1,0:T(8,128)S(1)} %copy-done.5, bf16[2,384,256]{2,1,0:T(8,128)(2,1)S(1)} %copy-done.4, bf16[2,512,512]{2,1,0:T(8,128)(2,1)S(1)} %copy-done, bf16[2,256,256]{2,1,0:T(8,128)(2,1)S(1)} %copy-done.7, f32[32,32,128]{2,1,0:T(8,128)S(1)} %copy-done.2, ...), custom_call_target="tpu_custom_call" | custom-call | tf_op jit(solution)/shard_map/pallas_call | solution.py:383
  40.6 0.0 copy-done.1
  40.6 0.0 copy-done.3
  40.6 0.0 copy-done.6
  40.6 0.0 copy-done.8
  40.6 0.0 copy-done.9
  40.6 0.0 copy-done.13
  40.6 0.0 copy-start.10
  40.7 1.0 %copy-done.10 = bf16[2,256,384]{2,1,0:T(8,128)(2,1)S(1)} copy-done((bf16[2,256,384]{2,1,0:T(8,128)(2,1)S(1)}, bf16[2,256,384]{2,1,0:T(8,128)(2,1)}, u32[]{:S(2)}) %copy-start.10) | copy-done | bytes 393240
  41.6 0.9 %copy-done.11 = bf16[2,256,256]{2,1,0:T(8,128)(2,1)S(1)} copy-done((bf16[2,256,256]{2,1,0:T(8,128)(2,1)S(1)}, bf16[2,256,256]{2,1,0:T(8,128)(2,1)}, u32[]{:S(2)}) %copy-start.11) | copy-done | bytes 262168
  42.6 10.1 %shard_map.101 = f32[4,32,32,32]{3,2,1,0:T(8,128)} custom-call(s32[4,3]{1,0:T(4,128)S(1)} %copy-done.13, f32[3,256,256]{2,1,0:T(8,128)S(1)} %get-tuple-element.7.first, f32[16,12,8,128]{3,2,1,0:T(8,128)S(1)} %get-tuple-element.8.held, bf16[2,384,256]{2,1,0:T(8,128)(2,1)S(1)} %copy-done.4, bf16[2,512,512]{2,1,0:T(8,128)(2,1)S(1)} %copy-done.1, ...), custom_call_target="tpu_custom_call" | custom-call | tf_op jit(solution)/shard_map/pallas_call | solution.py:404
  (6 shorter events, 0.0 us)
Async XLA Ops:
  0.0 1.2 %copy-start = (bf16[2,512,512]{2,1,0:T(8,128)(2,1)S(1)}, bf16[2,512,512]{2,1,0:T(8,128)(2,1)}, u32[]{:S(2)}) copy-start(bf16[2,512,512]{2,1,0:T(8,128)(2,1)} %constant.17.clone.along_z) | copy-start | bytes 3145732
  1.2 1.0 %copy-start.2 = (f32[32,32,128]{2,1,0:T(8,128)S(1)}, f32[32,32,128]{2,1,0:T(8,128)}, u32[]{:S(2)}) copy-start(f32[32,32,128]{2,1,0:T(8,128)} %constant.22.clone.weight3) | copy-start | bytes 1572868
  2.3 1.0 %copy-start.4 = (bf16[2,384,256]{2,1,0:T(8,128)(2,1)S(1)}, bf16[2,384,256]{2,1,0:T(8,128)(2,1)}, u32[]{:S(2)}) copy-start(bf16[2,384,256]{2,1,0:T(8,128)(2,1)} %constant.16.clone.along_y) | copy-start | bytes 1179652
  3.3 1.2 %copy-start.5 = (f32[2,8,32,512]{3,2,1,0:T(8,128)S(1)}, f32[2,8,32,512]{3,2,1,0:T(8,128)}, u32[]{:S(2)}) copy-start(f32[2,8,32,512]{3,2,1,0:T(8,128)} %volume.1) | copy-start | bytes 3145732
  4.5 0.9 %copy-start.7 = (bf16[2,256,256]{2,1,0:T(8,128)(2,1)S(1)}, bf16[2,256,256]{2,1,0:T(8,128)(2,1)}, u32[]{:S(2)}) copy-start(bf16[2,256,256]{2,1,0:T(8,128)(2,1)} %constant.18.clone.along_x) | copy-start | bytes 786436
  5.4 0.9 %copy-start.12 = (s32[512,1]{1,0:T(8,128)S(1)}, s32[512,1]{1,0:T(8,128)}, u32[]{:S(2)}) copy-start(s32[512,1]{1,0:T(8,128)} %constant.26.row_key) | copy-start | bytes 6148
  6.4 34.2 %copy-start.1 = (bf16[2,512,512]{2,1,0:T(8,128)(2,1)S(1)}, bf16[2,512,512]{2,1,0:T(8,128)(2,1)}, u32[]{:S(2)}) copy-start(bf16[2,512,512]{2,1,0:T(8,128)(2,1)} %constant.17.clone.along_z) | copy-start | bytes 3145732
  6.4 34.2 %copy-start.3 = (f32[32,32,128]{2,1,0:T(8,128)S(1)}, f32[32,32,128]{2,1,0:T(8,128)}, u32[]{:S(2)}) copy-start(f32[32,32,128]{2,1,0:T(8,128)} %constant.22.clone.weight3) | copy-start | bytes 1572868
  6.4 34.2 %copy-start.6 = (bf16[2,512,512]{2,1,0:T(8,128)(2,1)S(1)}, bf16[2,512,512]{2,1,0:T(8,128)(2,1)}, u32[]{:S(2)}) copy-start(bf16[2,512,512]{2,1,0:T(8,128)(2,1)} %constant.20.clone.back_z) | copy-start | bytes 3145732
  6.4 34.2 %copy-start.8 = (bf16[2,256,256]{2,1,0:T(8,128)(2,1)S(1)}, bf16[2,256,256]{2,1,0:T(8,128)(2,1)}, u32[]{:S(2)}) copy-start(bf16[2,256,256]{2,1,0:T(8,128)(2,1)} %constant.18.clone.along_x) | copy-start | bytes 786436
  6.4 34.2 %copy-start.9 = (s32[1024,1]{1,0:T(8,128)S(1)}, s32[1024,1]{1,0:T(8,128)}, u32[]{:S(2)}) copy-start(s32[1024,1]{1,0:T(8,128)} %constant.23.clone.row_key) | copy-start | bytes 12292
  6.4 34.2 %copy-start.13 = (s32[4,3]{1,0:T(4,128)S(1)}, s32[4,3]{1,0:T(4,128)}, u32[]{:S(2)}) copy-start(s32[4,3]{1,0:T(4,128)} %offsets.1) | copy-start | bytes 148
  40.6 1.0 %copy-start.10 = (bf16[2,256,384]{2,1,0:T(8,128)(2,1)S(1)}, bf16[2,256,384]{2,1,0:T(8,128)(2,1)}, u32[]{:S(2)}) copy-start(bf16[2,256,384]{2,1,0:T(8,128)(2,1)} %constant.21.clone.back_y) | copy-start | bytes 1179652
  41.6 0.9 %copy-start.11 = (bf16[2,256,256]{2,1,0:T(8,128)(2,1)S(1)}, bf16[2,256,256]{2,1,0:T(8,128)(2,1)}, u32[]{:S(2)}) copy-start(bf16[2,256,256]{2,1,0:T(8,128)(2,1)} %constant.19.clone.back_x) | copy-start | bytes 786436

commit v2 on v1

--- a/solution.py
+++ b/solution.py
@@ -182,22 +182,16 @@
     factor = 4.0 / W**1.5 / W**3
     parts = factor * np.stack([kept @ (weight * cosine), -(kept @ (weight * sine))]).reshape(2, KB, T, W)
     back_y = np.einsum("rbky,zs->zyrbsk", parts, unit).reshape(T * W, 2 * KB * T * T)
-    along_z = np.kron(np.block([[cosine, sine], [-sine, cosine]]), unit)
+    along_z = np.kron(np.concatenate([cosine, sine]), unit)
     four = np.eye(ZB)
     along_x = np.block([[np.kron(four, cosine), -np.kron(four, sine)], [np.kron(four, sine), np.kron(four, cosine)]])
     taper = 0.5 - 0.5 * np.cos(2.0 * np.pi * (index + 0.5) / W)
     lanes = np.tile(taper, ZB)
     weight3 = (taper[:, None, None] * taper[None, :, None] * lanes[None, None, :]).astype(np.float32)
-    lane = np.arange(128)
-    brick = np.arange(ZB)[:, None]
-    main = (brick * 4 + lane // W) * 64 + lane % W + H
-    edge = lane % 16
-    halo = (brick * 4 + lane % 64 // 16) * 64 + np.where(edge < H, edge, edge + W)
-    row_key = np.concatenate([main.reshape(-1), halo.reshape(-1)]).astype(np.int32)[:, None]
+    moved = np.einsum("qp,jk,xw->qjxkpw", four, four, np.eye(W)).reshape(512, 512).astype(ml_dtypes.bfloat16)
     return (
         halves(along_y), halves(along_z), halves(along_x),
-        halves(along_x.T), halves(along_z.T), halves(back_y),
-        weight3, row_key,
+        halves(along_x.T), halves(back_y), weight3, moved,
     )
 
 
@@ -244,10 +238,7 @@
         send[c, T:] = jnp.concatenate(parts, -1)
 
 
-def first_windows(held, row_key, field):
-    lane = lax.broadcasted_iota(jnp.int32, (1, 4 * 128), 1)
-    col_key = (lane // W % 4 * 4 + lane // 128) * 64 + lane % W + H
-    chosen = (row_key[0:512] == col_key).astype(jnp.float32).astype(jnp.bfloat16)
+def first_windows(held, chosen, field):
     rows = jnp.concatenate([held[4 * q : 4 * q + 4].reshape(W * T, 128) for q in range(ZB)], -1)
     high, low = split(rows)
     moved = mul(high, chosen) + mul(low, chosen)
@@ -255,14 +246,22 @@
         field[:, T * j : T * j + T, :] = moved[:, 128 * j : 128 * j + 128].reshape(W, T, 128)
 
 
-def second_windows(held, offsets, row_key, main, halo, spread, field):
-    lane = lax.broadcasted_iota(jnp.int32, (1, 4 * 128), 1)
-    brick = lane // W % 4
-    shift = jnp.zeros((1, 4 * 128), jnp.int32)
+def second_windows(held, offsets, main, halo, spread, field):
+    lane = lax.broadcasted_iota(jnp.int32, (1, 128), 1)
+    brick = lane >> 5
+    shift = jnp.zeros((1, 128), jnp.int32)
     for q in range(ZB):
         shift = jnp.where(brick == q, offsets[q, 2], shift)
-    col_key = (brick * 4 + lane // 128) * 64 + lane % W + H + shift
-    chosen = (row_key[...] == col_key).astype(jnp.float32).astype(jnp.bfloat16)
+    col_key = brick * 256 + (lane & 31) + H + shift
+    row = lax.broadcasted_iota(jnp.int32, (512, 128), 0)
+    owner = (row >> 7) * 256
+    edge = row & 15
+    main_key = owner + ((row >> 5) & 3) * 64 + (row & 31) + H
+    halo_key = owner + ((row >> 4) & 3) * 64 + jnp.where(edge < H, edge, edge + W)
+    chosen = jnp.concatenate([
+        jnp.concatenate([(key == col_key + 64 * j).astype(jnp.float32).astype(jnp.bfloat16) for j in range(4)], -1)
+        for key in (main_key, halo_key)
+    ], 0)
     depth = main.shape[0] - 2 * H
     for ref in (main, halo):
         ref[0:H] = jnp.zeros((H, T, 128), jnp.float32)
@@ -290,23 +289,42 @@
 
 def to_depth(field, weight3, along_y, mid):
     block = T * T
-    for zb in range(4):
-        tapered = field[T * zb : T * zb + T] * weight3[T * zb : T * zb + T]
-        part = from_left(along_y, tapered.reshape(T * W, 128))
-        for r in range(2):
-            for b in range(KB):
-                at = (r * KB + b) * block
-                mid[b, (r * 4 + zb) * block : (r * 4 + zb + 1) * block] = part[at : at + block]
+    for pair in range(2):
+        depths = (2 * pair, 2 * pair + 1)
+        tapered = [(field[T * zb : T * zb + T] * weight3[T * zb : T * zb + T]).reshape(T * W, 128) for zb in depths]
+        part = from_left(along_y, jnp.concatenate(tapered, -1))
+        for s, zb in enumerate(depths):
+            for r in range(2):
+                for b in range(KB):
+                    at = (r * KB + b) * block
+                    mid[b, zb * block : (zb + 1) * block, 128 * r : 128 * r + 128] = part[
+                        at : at + block, 128 * s : 128 * s + 128
+                    ]
+
+
+def cos_sin(along_z, lines):
+    both = from_left(along_z, lines)
+    cosine, sine = both[: W * T], both[W * T :]
+    return cosine[:, :128], cosine[:, 128:], sine[:, :128], sine[:, 128:]
 
 
 def to_spectrum(lines, along_z, along_x):
-    half = W * T
-    spec = from_left(along_z, lines)
-    return from_right(jnp.concatenate([spec[:half], spec[half:]], -1), along_x)
-
-
-def exchange(volume, along_y, along_z, along_x, weight3, row_key, spectrum, held_second,
-             send_first, send_second, held_first, field, mid, send_sem, recv_sem):
+    cos_re, cos_im, sin_re, sin_im = cos_sin(along_z, lines)
+    return from_right(jnp.concatenate([cos_re + sin_im, cos_im - sin_re], -1), along_x)
+
+
+def fetch(sources, targets, sems):
+    copies = [pltpu.make_async_copy(s, t, sems.at[i]) for i, (s, t) in enumerate(zip(sources, targets))]
+    for copy in copies:
+        copy.start()
+    return copies
+
+
+def exchange(voxels, *refs):
+    outside, (spectrum, held_second), refs = refs[:5], refs[5:7], refs[7:]
+    tables, (volume, send_first, send_second, held_first, field, mid, own_sem, table_sem, send_sem, recv_sem) = refs[:5], refs[5:]
+    along_y, along_z, along_x, weight3, chosen = tables
+    frames = fetch([voxels.at[f] for f in range(2)], [volume.at[f] for f in range(2)], own_sem)
     count = send_first.shape[0]
     me = lax.axis_index("brick")
     steps = sorted(range(1, count), key=lambda k: (abs(k - count // 2), k))
@@ -315,6 +333,7 @@
         pl.semaphore_signal(
             barrier, inc=1, device_id={"brick": lax.rem(me + k, count)}, device_id_type=pl.DeviceIdType.MESH
         )
+    frames[0].wait()
     pack_first(volume, send_first)
     pl.semaphore_wait(barrier, count - 1)
 
@@ -336,11 +355,14 @@
         return copies
 
     early = start(0, send_first, held_first)
+    frames[1].wait()
     pack_second(volume, send_second)
     late = start(1, send_second, held_second)
+    for copy in fetch(outside, tables, table_sem):
+        copy.wait()
     for copy in early:
         copy.wait()
-    first_windows(held_first, row_key, field)
+    first_windows(held_first, chosen[...], field)
     to_depth(field, weight3, along_y, mid)
     for b in range(KB):
         spectrum[b] = to_spectrum(mid[b], along_z, along_x)
@@ -348,9 +370,15 @@
         copy.wait()
 
 
-def correlate(offsets, first, held, along_y, along_z, along_x, back_x, back_z, back_y, weight3, row_key, out,
-              main, halo, spread, field, mid, back):
-    second_windows(held, offsets, row_key, main, halo, spread, field)
+def correlate(first, held, *refs):
+    outside, out, refs = refs[:7], refs[7], refs[8:]
+    inside, (main, halo, spread, field, mid, back, sems) = refs[:7], refs[7:]
+    copies = fetch(outside, inside, sems)
+    offsets, along_y, along_z, along_x, back_x, back_y, weight3 = inside
+    copies[0].wait()
+    second_windows(held, offsets, main, halo, spread, field)
+    for copy in copies[1:]:
+        copy.wait()
     to_depth(field, weight3, along_y, mid)
     block = T * T
     for b in range(KB):
@@ -360,15 +388,19 @@
         real_part = first_re * second_re + first_im * second_im
         imag_part = first_re * second_im - first_im * second_re
         lines = from_right(jnp.concatenate([real_part, imag_part], -1), back_x)
-        part = from_left(back_z, jnp.concatenate([lines[:, :128], lines[:, 128:]], 0))
-        for r in range(2):
+        cos_re, cos_im, sin_re, sin_im = cos_sin(along_z, lines)
+        for r, part in enumerate((cos_re - sin_im, cos_im + sin_re)):
+            at = (r * KB + b) * block
             for zb in range(4):
-                at = (r * 4 + zb) * block
-                back[zb, (r * KB + b) * block : (r * KB + b + 1) * block] = part[at : at + block]
-    for zb in range(4):
-        result = from_left(back_y, back[zb]).reshape(T, W, 128)
-        for q in range(ZB):
-            out[q, T * zb : T * zb + T] = result[:, :, W * q : W * q + W]
+                half = 128 * (zb % 2)
+                back[zb // 2, at : at + block, half : half + 128] = part[zb * block : (zb + 1) * block]
+    for pair in range(2):
+        results = from_left(back_y, back[pair])
+        for s in range(2):
+            zb = 2 * pair + s
+            result = results[:, 128 * s : 128 * s + 128].reshape(T, W, 128)
+            for q in range(ZB):
+                out[q, T * zb : T * zb + T] = result[:, :, W * q : W * q + W]
 
 
 def two_frames(volume, offsets):
@@ -377,45 +409,56 @@
     depth = slabs * planes
     rows = planes + planes // 2
     vmem = pl.BlockSpec(memory_space=pltpu.VMEM)
-    along_y, along_z, along_x, back_x, back_z, back_y, weight3, row_key = map(jnp.asarray, fixed_tables())
+    hbm = pl.BlockSpec(memory_space=pltpu.HBM)
+    tables = [jnp.asarray(table) for table in fixed_tables()]
+    along_y, along_z, along_x, back_x, back_y, weight3, moved = tables
+    early = (along_y, along_z, along_x, weight3, moved)
+    late = (along_y, along_z, along_x, back_x, back_y, weight3)
     field = pltpu.VMEM((W, W, 128), jnp.float32)
-    mid = pltpu.VMEM((KB, 2 * W * T, 128), jnp.float32)
+    mid = pltpu.VMEM((KB, W * T, 256), jnp.float32)
     first, held = pl.pallas_call(
         exchange,
         out_shape=[
             jax.ShapeDtypeStruct((KB, W * T, 256), jnp.float32),
             jax.ShapeDtypeStruct((slabs, rows, T, 128), jnp.float32),
         ],
-        in_specs=[vmem] * 6,
+        in_specs=[hbm] * (1 + len(early)),
         out_specs=[vmem] * 2,
         scratch_shapes=[
+            *[pltpu.VMEM(table.shape, table.dtype) for table in early],
+            pltpu.VMEM(volume.shape, jnp.float32),
             pltpu.VMEM((slabs, planes, T, 128), jnp.float32),
             pltpu.VMEM((slabs, rows, T, 128), jnp.float32),
             pltpu.VMEM((slabs, planes, T, 128), jnp.float32),
             field,
             mid,
+            pltpu.SemaphoreType.DMA((2,)),
+            pltpu.SemaphoreType.DMA((len(early),)),
             pltpu.SemaphoreType.DMA((2, slabs)),
             pltpu.SemaphoreType.DMA((2, slabs)),
         ],
         compiler_params=pltpu.CompilerParams(
-            collective_id=0, has_side_effects=True, vmem_limit_bytes=32 << 20
+            collective_id=0, has_side_effects=True, vmem_limit_bytes=63 << 20
         ),
-    )(volume, along_y, along_z, along_x, weight3, row_key[:512])
+    )(volume, *early)
     return pl.pallas_call(
         correlate,
         out_shape=jax.ShapeDtypeStruct((ZB, W, W, W), jnp.float32),
-        in_specs=[pl.BlockSpec(memory_space=pltpu.SMEM)] + [vmem] * 10,
+        in_specs=[vmem] * 2 + [hbm] * (1 + len(late)),
         out_specs=vmem,
         scratch_shapes=[
+            pltpu.SMEM(offsets.shape, jnp.int32),
+            *[pltpu.VMEM(table.shape, table.dtype) for table in late],
             pltpu.VMEM((depth + 2 * H, T, 128), jnp.float32),
             pltpu.VMEM((depth + 2 * H, T, 128), jnp.float32),
             pltpu.VMEM((W + 2 * H, W + 2 * H, 128), jnp.float32),
             field,
             mid,
-            pltpu.VMEM((4, 2 * KB * T * T, 128), jnp.float32),
+            pltpu.VMEM((2, 2 * KB * T * T, 256), jnp.float32),
+            pltpu.SemaphoreType.DMA((1 + len(late),)),
         ],
-        compiler_params=pltpu.CompilerParams(vmem_limit_bytes=32 << 20),
-    )(offsets, first, held, along_y, along_z, along_x, back_x, back_z, back_y, weight3, row_key)
+        compiler_params=pltpu.CompilerParams(vmem_limit_bytes=63 << 20),
+    )(first, held, offsets, *late)
 
 
 def per_device(volume, offsets):

time: 53.1 us -> 45 us (0.85)
  local copies, waits for them, and re-layouts: 8.35 us -> 0 us
    unnamed x28 -> x0, local copies, waits for them, and re-layouts: 8.35 us -> none
    pallas_call x1, Pallas kernels: 34.2 us -> 34.9 us  [two_frames(): pl.pallas_call(exchange, out_shape=[jax.ShapeDtypeStruct((KB, W * T, 256)...]
where the time goes in v2:
time: 45 us; the launch traced here: 44.8 us
  Pallas kernels  44.8 us (100%)
    pallas_call x1, Pallas kernels, two_frames(): pl.pallas_call(exchange, out_shape=[jax.ShapeDtypeStruct((KB, W * T, 256)...  34.9 us
    pallas_call x1, Pallas kernels, two_frames(): pl.pallas_call(correlate, out_shape=jax.ShapeDtypeStruct((ZB, W, W, W), j...  9.82 us

profile of v2, /device:TPU:0, one launch (start us, length us, event | category | flops | bytes accessed | tf_op | source)
XLA Modules:
  0.0 44.8 jit_solution(11734217552322617516)
XLA Ops:
  0.0 34.9 %shard_map.91 = (f32[3,256,256]{2,1,0:T(8,128)}, f32[16,12,8,128]{3,2,1,0:T(8,128)}) custom-call(f32[2,8,32,512]{3,2,1,0:T(8,128)} %voxels.1, bf16[2,384,256]{2,1,0:T(8,128)(2,1)} %constant.14.clone.refs_0_.refs_1_, bf16[2,512,256]{2,1,0:T(8,128)(2,1)} %constant.15.clone.refs_1_.refs_2_, bf16[2,256,256]{2,1,0:T(8,128)(2,1)} %constant.16.clone.refs_2_.refs_3_, ...), custom_call_target="tpu_custom_call" | custom-call | tf_op jit(solution)/shard_map/pallas_call | solution.py:419
  35.0 9.8 %shard_map.92 = f32[4,32,32,32]{3,2,1,0:T(8,128)} custom-call(f32[3,256,256]{2,1,0:T(8,128)} %get-tuple-element.7.first, f32[16,12,8,128]{3,2,1,0:T(8,128)} %get-tuple-element.8.held, s32[4,3]{1,0:T(4,128)} %refs_0_.2, bf16[2,384,256]{2,1,0:T(8,128)(2,1)} %constant.14.clone.refs_0_.refs_1_, bf16[2,512,256]{2,1,0:T(8,128)(2,1)} %constant.15.clone.refs_1_.refs_2_, ...), custom_call_target="tpu_custom_call" | custom-call | tf_op jit(solution)/shard_map/pallas_call | solution.py:444

commit v3 on v2

--- a/solution.py
+++ b/solution.py
@@ -321,8 +321,8 @@
 
 
 def exchange(voxels, *refs):
-    outside, (spectrum, held_second), refs = refs[:5], refs[5:7], refs[7:]
-    tables, (volume, send_first, send_second, held_first, field, mid, own_sem, table_sem, send_sem, recv_sem) = refs[:5], refs[5:]
+    outside, (spectrum_out, held_second), refs = refs[:5], refs[5:7], refs[7:]
+    tables, (volume, send_first, send_second, held_first, field, mid, spectrum, own_sem, table_sem, send_sem, recv_sem) = refs[:5], refs[5:]
     along_y, along_z, along_x, weight3, chosen = tables
     frames = fetch([voxels.at[f] for f in range(2)], [volume.at[f] for f in range(2)], own_sem)
     count = send_first.shape[0]
@@ -351,8 +351,9 @@
             )
             copy.start()
             copies.append(copy)
-        held[pl.ds(me, 1)] = send[pl.ds(me, 1)]
-        return copies
+        own = pltpu.make_async_copy(send.at[me], held.at[me], send_sem.at[f, 0])
+        own.start()
+        return copies + [own]
 
     early = start(0, send_first, held_first)
     frames[1].wait()
@@ -366,15 +367,17 @@
     to_depth(field, weight3, along_y, mid)
     for b in range(KB):
         spectrum[b] = to_spectrum(mid[b], along_z, along_x)
+    late.append(pltpu.make_async_copy(spectrum, spectrum_out, recv_sem.at[0, 0]))
+    late[-1].start()
     for copy in late:
         copy.wait()
 
 
-def correlate(first, held, *refs):
-    outside, out, refs = refs[:7], refs[7], refs[8:]
-    inside, (main, halo, spread, field, mid, back, sems) = refs[:7], refs[7:]
+def correlate(held, *refs):
+    outside, out, refs = refs[:8], refs[8], refs[9:]
+    inside, (main, halo, spread, field, mid, back, done, sems, out_sems) = refs[:8], refs[8:]
     copies = fetch(outside, inside, sems)
-    offsets, along_y, along_z, along_x, back_x, back_y, weight3 = inside
+    offsets, along_y, along_z, along_x, back_x, back_y, weight3, first = inside
     copies[0].wait()
     second_windows(held, offsets, main, halo, spread, field)
     for copy in copies[1:]:
@@ -394,13 +397,19 @@
             for zb in range(4):
                 half = 128 * (zb % 2)
                 back[zb // 2, at : at + block, half : half + 128] = part[zb * block : (zb + 1) * block]
+    leaving = []
     for pair in range(2):
         results = from_left(back_y, back[pair])
         for s in range(2):
             zb = 2 * pair + s
             result = results[:, 128 * s : 128 * s + 128].reshape(T, W, 128)
             for q in range(ZB):
-                out[q, T * zb : T * zb + T] = result[:, :, W * q : W * q + W]
+                done[q, T * zb : T * zb + T] = result[:, :, W * q : W * q + W]
+        half = pl.ds(2 * T * pair, 2 * T)
+        leaving.append(pltpu.make_async_copy(done.at[:, half], out.at[:, half], out_sems.at[pair]))
+        leaving[-1].start()
+    for copy in leaving:
+        copy.wait()
 
 
 def two_frames(volume, offsets):
@@ -423,7 +432,7 @@
             jax.ShapeDtypeStruct((slabs, rows, T, 128), jnp.float32),
         ],
         in_specs=[hbm] * (1 + len(early)),
-        out_specs=[vmem] * 2,
+        out_specs=[hbm] * 2,
         scratch_shapes=[
             *[pltpu.VMEM(table.shape, table.dtype) for table in early],
             pltpu.VMEM(volume.shape, jnp.float32),
@@ -432,6 +441,7 @@
             pltpu.VMEM((slabs, planes, T, 128), jnp.float32),
             field,
             mid,
+            pltpu.VMEM((KB, W * T, 256), jnp.float32),
             pltpu.SemaphoreType.DMA((2,)),
             pltpu.SemaphoreType.DMA((len(early),)),
             pltpu.SemaphoreType.DMA((2, slabs)),
@@ -441,11 +451,12 @@
             collective_id=0, has_side_effects=True, vmem_limit_bytes=63 << 20
         ),
     )(volume, *early)
+    late += (first,)
     return pl.pallas_call(
         correlate,
         out_shape=jax.ShapeDtypeStruct((ZB, W, W, W), jnp.float32),
-        in_specs=[vmem] * 2 + [hbm] * (1 + len(late)),
-        out_specs=vmem,
+        in_specs=[vmem] + [hbm] * (1 + len(late)),
+        out_specs=hbm,
         scratch_shapes=[
             pltpu.SMEM(offsets.shape, jnp.int32),
             *[pltpu.VMEM(table.shape, table.dtype) for table in late],
@@ -455,10 +466,12 @@
             field,
             mid,
             pltpu.VMEM((2, 2 * KB * T * T, 256), jnp.float32),
+            pltpu.VMEM((ZB, W, W, W), jnp.float32),
             pltpu.SemaphoreType.DMA((1 + len(late),)),
+            pltpu.SemaphoreType.DMA((2,)),
         ],
         compiler_params=pltpu.CompilerParams(vmem_limit_bytes=63 << 20),
-    )(first, held, offsets, *late)
+    )(held, offsets, *late)
 
 
 def per_device(volume, offsets):

time: 45 us -> 43.6 us (0.969)
  Pallas kernels: 44.8 us -> 43.4 us
    pallas_call x1, Pallas kernels: 34.9 us -> 33.9 us  [two_frames(): pl.pallas_call(exchange, out_shape=[jax.ShapeDtypeStruct((KB, W * T, 256)...]
where the time goes in v3:
time: 43.6 us; the launch traced here: 43.4 us
  Pallas kernels  43.4 us (100%)
    pallas_call x1, Pallas kernels, two_frames(): pl.pallas_call(exchange, out_shape=[jax.ShapeDtypeStruct((KB, W * T, 256)...  33.9 us
    pallas_call x1, Pallas kernels, two_frames(): pl.pallas_call(correlate, out_shape=jax.ShapeDtypeStruct((ZB, W, W, W), j...  9.48 us

profile of v3, /device:TPU:0, one launch (start us, length us, event | category | flops | bytes accessed | tf_op | source)
XLA Modules:
  0.0 43.4 jit_solution(16905975617906740355)
XLA Ops:
  0.0 33.9 %shard_map.91 = (f32[3,256,256]{2,1,0:T(8,128)}, f32[16,12,8,128]{3,2,1,0:T(8,128)}) custom-call(f32[2,8,32,512]{3,2,1,0:T(8,128)} %voxels.1, bf16[2,384,256]{2,1,0:T(8,128)(2,1)} %constant.14.clone.refs_0_.refs_1_, bf16[2,512,256]{2,1,0:T(8,128)(2,1)} %constant.15.clone.refs_1_.refs_2_, bf16[2,256,256]{2,1,0:T(8,128)(2,1)} %constant.16.clone.refs_2_.refs_3_, ...), custom_call_target="tpu_custom_call" | custom-call | tf_op jit(solution)/shard_map/pallas_call | solution.py:428
  33.9 9.5 %shard_map.92 = f32[4,32,32,32]{3,2,1,0:T(8,128)} custom-call(f32[16,12,8,128]{3,2,1,0:T(8,128)} %get-tuple-element.7.held, s32[4,3]{1,0:T(4,128)} %refs_0_.2, bf16[2,384,256]{2,1,0:T(8,128)(2,1)} %constant.14.clone.refs_0_.refs_1_, bf16[2,512,256]{2,1,0:T(8,128)(2,1)} %constant.15.clone.refs_1_.refs_2_, ...), custom_call_target="tpu_custom_call" | custom-call | tf_op jit(solution)/shard_map/pallas_call | solution.py:455
